TPU v7x, 256 devices: a whole 4x4x8 slice. The times are simulated.
256 devices in a mesh: dp: 4 (over y_hi, core), ctx: 64 (over z, y_lo, x).
Axes of the slice: x: 4, y: 4 (y_hi: 2, y_lo: 2; y = y_hi * 2 + y_lo), z: 8, core: 2. Of those that a mesh axis runs over, the one named last changes fastest.
Arguments:
- tokens: bfloat16 [4, 10240, 4096], P('dp', 'ctx'), may hold values from -6 to 6
- w_qkv: bfloat16 [4096, 5120], P('dp'), may hold values from -0.09375 to 0.09375
- col_scale: float32 [5120], replicated, may hold values from 0.4 to 1.6
- doc_ids: int32 [4, 10240], P('dp', 'ctx'), may hold values from 0 to 7, never falling along the last dimension, each value on 1 to 2560 neighbouring positions
Outputs:
- attended: bfloat16 [4, 10240, 4096], P('dp', 'ctx')
Inputs may be any that keep to these rules, and one draw needn't show every extreme that they name: `doc_ids`: along each sequence the ids never fall; every document holds at most 2560 tokens and some document holds exactly 2560.
All inputs are finite; a program needn't handle non-finite values.
Results may differ from a plain program's by a relative error of at most 0.04.
Values may be sent and summed in bfloat16 or wider, within the bound.
A program may use at most 192 MiB of HBM per device.

v0:
```python
import math
import jax
import jax.numpy as jnp
from jax import lax
from jax.sharding import PartitionSpec as P

QH = 32
KVH = 4
HD = 128


def shifted(block, axis, distance):
    devices = range(lax.axis_size(axis))
    route = [(i - distance, i) for i in devices if i - distance in devices]
    return lax.ppermute(block, axis, route)


def rotate(vectors, positions):
    half_width = vectors.shape[-1] // 2
    freqs = jnp.exp(
        -math.log(500000.0) * 2.0 * jnp.arange(half_width, dtype=jnp.float32) / vectors.shape[-1]
    )
    angles = positions.astype(jnp.float32)[:, None] * freqs[None, :]
    cosine = jnp.cos(angles)[:, None, :]
    sine = jnp.sin(angles)[:, None, :]
    first = vectors[..., :half_width]
    second = vectors[..., half_width:]
    return jnp.concatenate(
        [first * cosine - second * sine, second * cosine + first * sine], axis=-1
    )


def local(tokens, w_qkv, col_scale, doc_ids):
    tok_rows = tokens.shape[1]
    groups = QH // KVH
    score_scale = 1.0 / math.sqrt(HD)
    spread = lax.all_to_all(tokens, "dp", split_axis=2, concat_axis=0, tiled=True)
    summed = lax.psum_scatter(
        jnp.einsum("btd,dc->btc", spread, w_qkv, preferred_element_type=jnp.float32).astype(
            jnp.bfloat16
        ),
        "dp",
        scatter_dimension=0,
        tiled=True,
    ).astype(jnp.float32)
    qkv = summed[0] * col_scale
    base = lax.axis_index("ctx") * tok_rows
    positions = base + jnp.arange(tok_rows, dtype=jnp.int32)
    queries = rotate(qkv[:, : QH * HD].reshape(tok_rows, QH, HD), positions).astype(jnp.bfloat16)
    queries = queries.reshape(tok_rows, KVH, groups, HD)
    keys = rotate(qkv[:, QH * HD : (QH + KVH) * HD].reshape(tok_rows, KVH, HD), positions).astype(
        jnp.bfloat16
    )
    values = qkv[:, (QH + KVH) * HD :].reshape(tok_rows, KVH, HD).astype(jnp.bfloat16)
    query_docs = doc_ids[0]

    def attend(state, key_rows, value_rows, key_pos, key_docs):
        mask = (
            (key_docs[None, :] == query_docs[:, None])
            & (key_pos[None, :] <= positions[:, None])
            & (key_pos[None, :] >= 0)
        )
        run_max, run_sum, run_acc = state
        scores = (
            jnp.einsum("tgjd,sgd->gjts", queries, key_rows, preferred_element_type=jnp.float32)
            * score_scale
        )
        scores = jnp.where(mask[None, None], scores, -jnp.inf)
        new_max = jnp.maximum(run_max, jnp.max(scores, axis=-1))
        factor = jnp.exp(run_max - new_max)
        expo = jnp.exp(scores - new_max[..., None])
        new_sum = run_sum * factor + jnp.sum(expo, axis=-1)
        new_acc = run_acc * factor[..., None] + jnp.einsum(
            "gjts,sgd->gjtd",
            expo.astype(jnp.bfloat16),
            value_rows,
            preferred_element_type=jnp.float32,
        )
        return (new_max, new_sum, new_acc)

    state = (
        jnp.full((KVH, groups, tok_rows), -1e30, jnp.float32),
        jnp.zeros((KVH, groups, tok_rows), jnp.float32),
        jnp.zeros((KVH, groups, tok_rows, HD), jnp.float32),
    )
    state = attend(state, keys, values, positions, query_docs)
    span = min(16, lax.axis_size("ctx") // 2)

    def turn(step, carry):
        block, current = carry
        block = shifted((block[0], block[1], block[2]), "ctx", 1)
        key_pos = positions - (step + 1) * tok_rows
        current = attend(current, block[0], block[1], key_pos, block[2])
        return (block, current)

    final = lax.fori_loop(0, span, turn, ((keys, values, query_docs), state))
    state = final[1]
    run_max, run_sum, run_acc = state
    mixed = run_acc / run_sum[..., None]
    return mixed.transpose(2, 0, 1, 3).reshape(1, tok_rows, QH * HD).astype(jnp.bfloat16)


def solution(mesh):
    return jax.shard_map(
        local,
        mesh=mesh,
        in_specs=(P("dp", "ctx", None), P("dp", None), P(), P("dp", "ctx")),
        out_specs=P("dp", "ctx", None),
        check_vma=False,
    )
```

profile of v0, /device:TPU:72, one launch (start us, length us, event | category | flops | bytes accessed | tf_op | source)
XLA Modules:
  0.0 545.9 jit_solution(9981145204996563690)
XLA Ops:
  6.5 9.8 %copy.25 = bf16[1,160,4096]{1,0,2:T(2,128)(2,1)} copy(bf16[1,160,4096]{2,1,0:T(8,128)(2,1)} %param.6) | data formatting | bytes 2621440 | tf_op args[0]
  16.9 23.6 %reduce = bf16[4096,160]{1,0:T(8,128)(2,1)S(1)} reduce(bf16[4096,1,160]{2,1,0:T(2,128)(2,1)} %bitcast.91, bf16[]{:T(256)} %broadcast.243), dimensions={1}, to_apply=%bitcast.66.reduce_sub_computation | reduce | bytes 2621442
  40.5 3.2 reshape.275
  43.7 22.1 %all_to_all.18 = bf16[4,2,81920]{2,1,0:T(2,128)(2,1)S(1)} all-to-all(bf16[4,2,81920]{2,1,0:T(2,128)(2,1)S(1)} %reshape.275), channel_id=1, replica_groups=mesh['dp'=4,'ctx'=64] {'dp'}, dimensions={0} | all-to-all | bytes 2621440 | tf_op jit(solution)/shard_map/all_to_all | solution.py:37
  65.9 4.5 reshape.276
  74.2 12.8 %fusion.20 = bf16[4,160,5120]{2,1,0:T(8,128)(2,1)} fusion(bf16[1024,5120]{1,0:T(8,128)(2,1)} %param.7, bf16[1,160,4,1024]{3,1,2,0:T(8,128)(2,1)S(1)} %copy.27), kind=kOutput, calls=%fused_computation.25 | convolution fusion | flops 6714163200 | bytes 18350080 | tf_op jit(solution)/shard_map/btd,dc->btc/dot_general | solution.py:39
  88.3 70.8 %reduce-scatter.2.cloned.1.call-done = bf16[1,160,5120]{2,1,0:T(8,128)(2,1)} async-done(((bf16[4,160,5120]{2,1,0:T(8,128)(2,1)}), bf16[1,160,5120]{2,1,0:T(8,128)(2,1)}) %reduce-scatter.2.cloned.1.call-update) | async-done | bytes 1638416 | tf_op jit(solution)/shard_map/reduce_scatter | solution.py:38
  174.0 362.3 %while.24 = (s32[]{:T(128)}, bf16[160,4,128]{2,0,1:T(8,128)(2,1)S(1)}, bf16[160,4,128]{2,0,1:T(8,128)(2,1)S(1)}, s32[160]{0:T(256)S(1)}, f32[4,8,160]{2,1,0:T(8,...) while((s32[]{:T(128)}, ...), condition=%wide.region_6.7_spmd.clone, body=%wide.region_3.6_spmd.clone.sunk | while | flops 429865760 | bytes 19116104 | solution.py:96
  174.2 3.4 collective-permute-start.2
  177.6 3.4 collective-permute-start.1
  181.0 3.1 collective-permute-start
  184.2 6.5 %collective-permute-done = bf16[160,4,128]{2,0,1:T(8,128)(2,1)S(1)} collective-permute-done((bf16[160,4,128]{2,0,1:T(8,128)(2,1)S(1)}, bf16[160,4,128]{2,0,1:T(8,128)(2,1)S(1)}, u32[]{:S(2)}, u32[]{:S(2)}) %collective-permute-start) | collective-permute-done | bytes 163872 | tf_op jit(solution)/shard_map/while/body/eval_jaxpr/ppermute | solution.py:15
  202.3 3.8 collective-permute-start
  206.3 5.6 %collective-permute-done = bf16[160,4,128]{2,0,1:T(8,128)(2,1)S(1)} collective-permute-done((bf16[160,4,128]{2,0,1:T(8,128)(2,1)S(1)}, bf16[160,4,128]{2,0,1:T(8,128)(2,1)S(1)}, u32[]{:S(2)}, u32[]{:S(2)}) %collective-permute-start) | collective-permute-done | bytes 163872 | tf_op jit(solution)/shard_map/while/body/eval_jaxpr/ppermute | solution.py:15
  215.5 3.1 multiply_add_fusion.5
  218.6 3.4 collective-permute-start.2
  222.0 4.4 collective-permute-start.1
  229.6 6.2 %collective-permute-done = bf16[160,4,128]{2,0,1:T(8,128)(2,1)S(1)} collective-permute-done((bf16[160,4,128]{2,0,1:T(8,128)(2,1)S(1)}, bf16[160,4,128]{2,0,1:T(8,128)(2,1)S(1)}, u32[]{:S(2)}, u32[]{:S(2)}) %collective-permute-start) | collective-permute-done | bytes 163872 | tf_op jit(solution)/shard_map/while/body/eval_jaxpr/ppermute | solution.py:15
  239.3 3.1 multiply_add_fusion.5
  244.3 4.1 collective-permute-start.1
  250.9 6.9 %collective-permute-done = bf16[160,4,128]{2,0,1:T(8,128)(2,1)S(1)} collective-permute-done((bf16[160,4,128]{2,0,1:T(8,128)(2,1)S(1)}, bf16[160,4,128]{2,0,1:T(8,128)(2,1)S(1)}, u32[]{:S(2)}, u32[]{:S(2)}) %collective-permute-start) | collective-permute-done | bytes 163872 | tf_op jit(solution)/shard_map/while/body/eval_jaxpr/ppermute | solution.py:15
  266.4 3.4 collective-permute-start.1
  272.2 7.0 %collective-permute-done = bf16[160,4,128]{2,0,1:T(8,128)(2,1)S(1)} collective-permute-done((bf16[160,4,128]{2,0,1:T(8,128)(2,1)S(1)}, bf16[160,4,128]{2,0,1:T(8,128)(2,1)S(1)}, u32[]{:S(2)}, u32[]{:S(2)}) %collective-permute-start) | collective-permute-done | bytes 163872 | tf_op jit(solution)/shard_map/while/body/eval_jaxpr/ppermute | solution.py:15
  287.8 3.5 collective-permute-start.1
  291.3 3.5 collective-permute-start
  295.0 5.6 %collective-permute-done = bf16[160,4,128]{2,0,1:T(8,128)(2,1)S(1)} collective-permute-done((bf16[160,4,128]{2,0,1:T(8,128)(2,1)S(1)}, bf16[160,4,128]{2,0,1:T(8,128)(2,1)S(1)}, u32[]{:S(2)}, u32[]{:S(2)}) %collective-permute-start) | collective-permute-done | bytes 163872 | tf_op jit(solution)/shard_map/while/body/eval_jaxpr/ppermute | solution.py:15
  307.3 4.4 collective-permute-start.2
  311.7 4.4 collective-permute-start.1
  318.2 7.2 %collective-permute-done = bf16[160,4,128]{2,0,1:T(8,128)(2,1)S(1)} collective-permute-done((bf16[160,4,128]{2,0,1:T(8,128)(2,1)S(1)}, bf16[160,4,128]{2,0,1:T(8,128)(2,1)S(1)}, u32[]{:S(2)}, u32[]{:S(2)}) %collective-permute-start) | collective-permute-done | bytes 163872 | tf_op jit(solution)/shard_map/while/body/eval_jaxpr/ppermute | solution.py:15
  334.9 4.4 collective-permute-start.1
  341.5 7.2 %collective-permute-done = bf16[160,4,128]{2,0,1:T(8,128)(2,1)S(1)} collective-permute-done((bf16[160,4,128]{2,0,1:T(8,128)(2,1)S(1)}, bf16[160,4,128]{2,0,1:T(8,128)(2,1)S(1)}, u32[]{:S(2)}, u32[]{:S(2)}) %collective-permute-start) | collective-permute-done | bytes 163872 | tf_op jit(solution)/shard_map/while/body/eval_jaxpr/ppermute | solution.py:15
  357.5 4.4 collective-permute-start.1
  364.0 7.2 %collective-permute-done = bf16[160,4,128]{2,0,1:T(8,128)(2,1)S(1)} collective-permute-done((bf16[160,4,128]{2,0,1:T(8,128)(2,1)S(1)}, bf16[160,4,128]{2,0,1:T(8,128)(2,1)S(1)}, u32[]{:S(2)}, u32[]{:S(2)}) %collective-permute-start) | collective-permute-done | bytes 163872 | tf_op jit(solution)/shard_map/while/body/eval_jaxpr/ppermute | solution.py:15
  379.9 4.0 collective-permute-start.1
  386.0 7.2 %collective-permute-done = bf16[160,4,128]{2,0,1:T(8,128)(2,1)S(1)} collective-permute-done((bf16[160,4,128]{2,0,1:T(8,128)(2,1)S(1)}, bf16[160,4,128]{2,0,1:T(8,128)(2,1)S(1)}, u32[]{:S(2)}, u32[]{:S(2)}) %collective-permute-start) | collective-permute-done | bytes 163872 | tf_op jit(solution)/shard_map/while/body/eval_jaxpr/ppermute | solution.py:15
  401.8 4.0 collective-permute-start.1
  408.0 7.2 %collective-permute-done = bf16[160,4,128]{2,0,1:T(8,128)(2,1)S(1)} collective-permute-done((bf16[160,4,128]{2,0,1:T(8,128)(2,1)S(1)}, bf16[160,4,128]{2,0,1:T(8,128)(2,1)S(1)}, u32[]{:S(2)}, u32[]{:S(2)}) %collective-permute-start) | collective-permute-done | bytes 163872 | tf_op jit(solution)/shard_map/while/body/eval_jaxpr/ppermute | solution.py:15
  423.8 4.0 collective-permute-start.1
  430.0 7.2 %collective-permute-done = bf16[160,4,128]{2,0,1:T(8,128)(2,1)S(1)} collective-permute-done((bf16[160,4,128]{2,0,1:T(8,128)(2,1)S(1)}, bf16[160,4,128]{2,0,1:T(8,128)(2,1)S(1)}, u32[]{:S(2)}, u32[]{:S(2)}) %collective-permute-start) | collective-permute-done | bytes 163872 | tf_op jit(solution)/shard_map/while/body/eval_jaxpr/ppermute | solution.py:15
  443.8 3.1 collective-permute-start.2
  447.0 4.4 collective-permute-start.1
  453.5 7.7 %collective-permute-done = bf16[160,4,128]{2,0,1:T(8,128)(2,1)S(1)} collective-permute-done((bf16[160,4,128]{2,0,1:T(8,128)(2,1)S(1)}, bf16[160,4,128]{2,0,1:T(8,128)(2,1)S(1)}, u32[]{:S(2)}, u32[]{:S(2)}) %collective-permute-start) | collective-permute-done | bytes 163872 | tf_op jit(solution)/shard_map/while/body/eval_jaxpr/ppermute | solution.py:15
  475.6 7.3 %collective-permute-done = bf16[160,4,128]{2,0,1:T(8,128)(2,1)S(1)} collective-permute-done((bf16[160,4,128]{2,0,1:T(8,128)(2,1)S(1)}, bf16[160,4,128]{2,0,1:T(8,128)(2,1)S(1)}, u32[]{:S(2)}, u32[]{:S(2)}) %collective-permute-start) | collective-permute-done | bytes 163872 | tf_op jit(solution)/shard_map/while/body/eval_jaxpr/ppermute | solution.py:15
  497.6 7.8 %collective-permute-done = bf16[160,4,128]{2,0,1:T(8,128)(2,1)S(1)} collective-permute-done((bf16[160,4,128]{2,0,1:T(8,128)(2,1)S(1)}, bf16[160,4,128]{2,0,1:T(8,128)(2,1)S(1)}, u32[]{:S(2)}, u32[]{:S(2)}) %collective-permute-start) | collective-permute-done | bytes 163872 | tf_op jit(solution)/shard_map/while/body/eval_jaxpr/ppermute | solution.py:15
  512.2 3.7 collective-permute-start.2
  515.9 4.4 collective-permute-start.1
  520.3 3.7 collective-permute-start
  524.2 5.4 collective-permute-done
  (292 shorter events, 182.7 us)
Async XLA Ops:
  6.5 152.5 %reduce-scatter.2.cloned.1.call-start = ((), (), s32[]{:S(2)}) async-start(), calls=%async_computation.2 | async-start | bytes 8192000 | tf_op jit(solution)/shard_map/reduce_scatter | solution.py:38
  174.2 9.9 %collective-permute-start.2 = (s32[160]{0:T(256)S(1)}, s32[160]{0:T(256)S(1)}, u32[]{:S(2)}, u32[]{:S(2)}) collective-permute-start(s32[160]{0:T(256)S(1)} %get-tuple-element.358), channel_id=1, source_target_pairs={{0,1},{1,2},{2,3},{3,4},{4,5},{5,6},{6,7},{7,8},{8,9},{9,10},{10,1... | collective-permute-start | bytes 1928 | tf_op jit(solution)/shard_map/while/body/eval_jaxpr/ppermute | solution.py:15
  177.6 16.7 %collective-permute-start.1 = (bf16[160,4,128]{2,0,1:T(8,128)(2,1)S(1)}, bf16[160,4,128]{2,0,1:T(8,128)(2,1)S(1)}, u32[]{:S(2)}, u32[]{:S(2)}) collective-permute-start(bf16[160,4,128]{2,0,1:T(8,128)(2,1)S(1)} %get-tuple-element.357), channel_id=1, source_target_pairs={{0,1},{1,2},{2,3},{3,4},{4,5},{5,6},{6,7},{7,8},{8,9},{9,10},{10,1... | collective-permute-start | bytes 491528 | tf_op jit(solution)/shard_map/while/body/eval_jaxpr/ppermute | solution.py:15
  181.0 9.8 %collective-permute-start = (bf16[160,4,128]{2,0,1:T(8,128)(2,1)S(1)}, bf16[160,4,128]{2,0,1:T(8,128)(2,1)S(1)}, u32[]{:S(2)}, u32[]{:S(2)}) collective-permute-start(bf16[160,4,128]{2,0,1:T(8,128)(2,1)S(1)} %get-tuple-element.356), channel_id=1, source_target_pairs={{0,1},{1,2},{2,3},{3,4},{4,5},{5,6},{6,7},{7,8},{8,9},{9,10},{10,1... | collective-permute-start | bytes 491528 | tf_op jit(solution)/shard_map/while/body/eval_jaxpr/ppermute | solution.py:15
  197.4 8.7 %collective-permute-start.2 = (s32[160]{0:T(256)S(1)}, s32[160]{0:T(256)S(1)}, u32[]{:S(2)}, u32[]{:S(2)}) collective-permute-start(s32[160]{0:T(256)S(1)} %get-tuple-element.358), channel_id=1, source_target_pairs={{0,1},{1,2},{2,3},{3,4},{4,5},{5,6},{6,7},{7,8},{8,9},{9,10},{10,1... | collective-permute-start | bytes 1928 | tf_op jit(solution)/shard_map/while/body/eval_jaxpr/ppermute | solution.py:15
  199.4 16.1 %collective-permute-start.1 = (bf16[160,4,128]{2,0,1:T(8,128)(2,1)S(1)}, bf16[160,4,128]{2,0,1:T(8,128)(2,1)S(1)}, u32[]{:S(2)}, u32[]{:S(2)}) collective-permute-start(bf16[160,4,128]{2,0,1:T(8,128)(2,1)S(1)} %get-tuple-element.357), channel_id=1, source_target_pairs={{0,1},{1,2},{2,3},{3,4},{4,5},{5,6},{6,7},{7,8},{8,9},{9,10},{10,1... | collective-permute-start | bytes 491528 | tf_op jit(solution)/shard_map/while/body/eval_jaxpr/ppermute | solution.py:15
  202.3 9.6 %collective-permute-start = (bf16[160,4,128]{2,0,1:T(8,128)(2,1)S(1)}, bf16[160,4,128]{2,0,1:T(8,128)(2,1)S(1)}, u32[]{:S(2)}, u32[]{:S(2)}) collective-permute-start(bf16[160,4,128]{2,0,1:T(8,128)(2,1)S(1)} %get-tuple-element.356), channel_id=1, source_target_pairs={{0,1},{1,2},{2,3},{3,4},{4,5},{5,6},{6,7},{7,8},{8,9},{9,10},{10,1... | collective-permute-start | bytes 491528 | tf_op jit(solution)/shard_map/while/body/eval_jaxpr/ppermute | solution.py:15
  218.6 10.8 %collective-permute-start.2 = (s32[160]{0:T(256)S(1)}, s32[160]{0:T(256)S(1)}, u32[]{:S(2)}, u32[]{:S(2)}) collective-permute-start(s32[160]{0:T(256)S(1)} %get-tuple-element.358), channel_id=1, source_target_pairs={{0,1},{1,2},{2,3},{3,4},{4,5},{5,6},{6,7},{7,8},{8,9},{9,10},{10,1... | collective-permute-start | bytes 1928 | tf_op jit(solution)/shard_map/while/body/eval_jaxpr/ppermute | solution.py:15
  222.0 17.3 %collective-permute-start.1 = (bf16[160,4,128]{2,0,1:T(8,128)(2,1)S(1)}, bf16[160,4,128]{2,0,1:T(8,128)(2,1)S(1)}, u32[]{:S(2)}, u32[]{:S(2)}) collective-permute-start(bf16[160,4,128]{2,0,1:T(8,128)(2,1)S(1)} %get-tuple-element.357), channel_id=1, source_target_pairs={{0,1},{1,2},{2,3},{3,4},{4,5},{5,6},{6,7},{7,8},{8,9},{9,10},{10,1... | collective-permute-start | bytes 491528 | tf_op jit(solution)/shard_map/while/body/eval_jaxpr/ppermute | solution.py:15
  226.4 9.3 %collective-permute-start = (bf16[160,4,128]{2,0,1:T(8,128)(2,1)S(1)}, bf16[160,4,128]{2,0,1:T(8,128)(2,1)S(1)}, u32[]{:S(2)}, u32[]{:S(2)}) collective-permute-start(bf16[160,4,128]{2,0,1:T(8,128)(2,1)S(1)} %get-tuple-element.356), channel_id=1, source_target_pairs={{0,1},{1,2},{2,3},{3,4},{4,5},{5,6},{6,7},{7,8},{8,9},{9,10},{10,1... | collective-permute-start | bytes 491528 | tf_op jit(solution)/shard_map/while/body/eval_jaxpr/ppermute | solution.py:15
  242.4 8.3 %collective-permute-start.2 = (s32[160]{0:T(256)S(1)}, s32[160]{0:T(256)S(1)}, u32[]{:S(2)}, u32[]{:S(2)}) collective-permute-start(s32[160]{0:T(256)S(1)} %get-tuple-element.358), channel_id=1, source_target_pairs={{0,1},{1,2},{2,3},{3,4},{4,5},{5,6},{6,7},{7,8},{8,9},{9,10},{10,1... | collective-permute-start | bytes 1928 | tf_op jit(solution)/shard_map/while/body/eval_jaxpr/ppermute | solution.py:15
  244.3 17.0 %collective-permute-start.1 = (bf16[160,4,128]{2,0,1:T(8,128)(2,1)S(1)}, bf16[160,4,128]{2,0,1:T(8,128)(2,1)S(1)}, u32[]{:S(2)}, u32[]{:S(2)}) collective-permute-start(bf16[160,4,128]{2,0,1:T(8,128)(2,1)S(1)} %get-tuple-element.357), channel_id=1, source_target_pairs={{0,1},{1,2},{2,3},{3,4},{4,5},{5,6},{6,7},{7,8},{8,9},{9,10},{10,1... | collective-permute-start | bytes 491528 | tf_op jit(solution)/shard_map/while/body/eval_jaxpr/ppermute | solution.py:15
  248.5 9.3 %collective-permute-start = (bf16[160,4,128]{2,0,1:T(8,128)(2,1)S(1)}, bf16[160,4,128]{2,0,1:T(8,128)(2,1)S(1)}, u32[]{:S(2)}, u32[]{:S(2)}) collective-permute-start(bf16[160,4,128]{2,0,1:T(8,128)(2,1)S(1)} %get-tuple-element.356), channel_id=1, source_target_pairs={{0,1},{1,2},{2,3},{3,4},{4,5},{5,6},{6,7},{7,8},{8,9},{9,10},{10,1... | collective-permute-start | bytes 491528 | tf_op jit(solution)/shard_map/while/body/eval_jaxpr/ppermute | solution.py:15
  264.5 7.6 %collective-permute-start.2 = (s32[160]{0:T(256)S(1)}, s32[160]{0:T(256)S(1)}, u32[]{:S(2)}, u32[]{:S(2)}) collective-permute-start(s32[160]{0:T(256)S(1)} %get-tuple-element.358), channel_id=1, source_target_pairs={{0,1},{1,2},{2,3},{3,4},{4,5},{5,6},{6,7},{7,8},{8,9},{9,10},{10,1... | collective-permute-start | bytes 1928 | tf_op jit(solution)/shard_map/while/body/eval_jaxpr/ppermute | solution.py:15
  266.4 16.3 %collective-permute-start.1 = (bf16[160,4,128]{2,0,1:T(8,128)(2,1)S(1)}, bf16[160,4,128]{2,0,1:T(8,128)(2,1)S(1)}, u32[]{:S(2)}, u32[]{:S(2)}) collective-permute-start(bf16[160,4,128]{2,0,1:T(8,128)(2,1)S(1)} %get-tuple-element.357), channel_id=1, source_target_pairs={{0,1},{1,2},{2,3},{3,4},{4,5},{5,6},{6,7},{7,8},{8,9},{9,10},{10,1... | collective-permute-start | bytes 491528 | tf_op jit(solution)/shard_map/while/body/eval_jaxpr/ppermute | solution.py:15
  269.8 9.3 %collective-permute-start = (bf16[160,4,128]{2,0,1:T(8,128)(2,1)S(1)}, bf16[160,4,128]{2,0,1:T(8,128)(2,1)S(1)}, u32[]{:S(2)}, u32[]{:S(2)}) collective-permute-start(bf16[160,4,128]{2,0,1:T(8,128)(2,1)S(1)} %get-tuple-element.356), channel_id=1, source_target_pairs={{0,1},{1,2},{2,3},{3,4},{4,5},{5,6},{6,7},{7,8},{8,9},{9,10},{10,1... | collective-permute-start | bytes 491528 | tf_op jit(solution)/shard_map/while/body/eval_jaxpr/ppermute | solution.py:15
  285.8 9.0 %collective-permute-start.2 = (s32[160]{0:T(256)S(1)}, s32[160]{0:T(256)S(1)}, u32[]{:S(2)}, u32[]{:S(2)}) collective-permute-start(s32[160]{0:T(256)S(1)} %get-tuple-element.358), channel_id=1, source_target_pairs={{0,1},{1,2},{2,3},{3,4},{4,5},{5,6},{6,7},{7,8},{8,9},{9,10},{10,1... | collective-permute-start | bytes 1928 | tf_op jit(solution)/shard_map/while/body/eval_jaxpr/ppermute | solution.py:15
  287.8 16.4 %collective-permute-start.1 = (bf16[160,4,128]{2,0,1:T(8,128)(2,1)S(1)}, bf16[160,4,128]{2,0,1:T(8,128)(2,1)S(1)}, u32[]{:S(2)}, u32[]{:S(2)}) collective-permute-start(bf16[160,4,128]{2,0,1:T(8,128)(2,1)S(1)} %get-tuple-element.357), channel_id=1, source_target_pairs={{0,1},{1,2},{2,3},{3,4},{4,5},{5,6},{6,7},{7,8},{8,9},{9,10},{10,1... | collective-permute-start | bytes 491528 | tf_op jit(solution)/shard_map/while/body/eval_jaxpr/ppermute | solution.py:15
  291.3 9.3 %collective-permute-start = (bf16[160,4,128]{2,0,1:T(8,128)(2,1)S(1)}, bf16[160,4,128]{2,0,1:T(8,128)(2,1)S(1)}, u32[]{:S(2)}, u32[]{:S(2)}) collective-permute-start(bf16[160,4,128]{2,0,1:T(8,128)(2,1)S(1)} %get-tuple-element.356), channel_id=1, source_target_pairs={{0,1},{1,2},{2,3},{3,4},{4,5},{5,6},{6,7},{7,8},{8,9},{9,10},{10,1... | collective-permute-start | bytes 491528 | tf_op jit(solution)/shard_map/while/body/eval_jaxpr/ppermute | solution.py:15
  307.3 10.8 %collective-permute-start.2 = (s32[160]{0:T(256)S(1)}, s32[160]{0:T(256)S(1)}, u32[]{:S(2)}, u32[]{:S(2)}) collective-permute-start(s32[160]{0:T(256)S(1)} %get-tuple-element.358), channel_id=1, source_target_pairs={{0,1},{1,2},{2,3},{3,4},{4,5},{5,6},{6,7},{7,8},{8,9},{9,10},{10,1... | collective-permute-start | bytes 1928 | tf_op jit(solution)/shard_map/while/body/eval_jaxpr/ppermute | solution.py:15
  311.7 17.3 %collective-permute-start.1 = (bf16[160,4,128]{2,0,1:T(8,128)(2,1)S(1)}, bf16[160,4,128]{2,0,1:T(8,128)(2,1)S(1)}, u32[]{:S(2)}, u32[]{:S(2)}) collective-permute-start(bf16[160,4,128]{2,0,1:T(8,128)(2,1)S(1)} %get-tuple-element.357), channel_id=1, source_target_pairs={{0,1},{1,2},{2,3},{3,4},{4,5},{5,6},{6,7},{7,8},{8,9},{9,10},{10,1... | collective-permute-start | bytes 491528 | tf_op jit(solution)/shard_map/while/body/eval_jaxpr/ppermute | solution.py:15
  316.1 9.3 %collective-permute-start = (bf16[160,4,128]{2,0,1:T(8,128)(2,1)S(1)}, bf16[160,4,128]{2,0,1:T(8,128)(2,1)S(1)}, u32[]{:S(2)}, u32[]{:S(2)}) collective-permute-start(bf16[160,4,128]{2,0,1:T(8,128)(2,1)S(1)} %get-tuple-element.356), channel_id=1, source_target_pairs={{0,1},{1,2},{2,3},{3,4},{4,5},{5,6},{6,7},{7,8},{8,9},{9,10},{10,1... | collective-permute-start | bytes 491528 | tf_op jit(solution)/shard_map/while/body/eval_jaxpr/ppermute | solution.py:15
  332.1 9.2 %collective-permute-start.2 = (s32[160]{0:T(256)S(1)}, s32[160]{0:T(256)S(1)}, u32[]{:S(2)}, u32[]{:S(2)}) collective-permute-start(s32[160]{0:T(256)S(1)} %get-tuple-element.358), channel_id=1, source_target_pairs={{0,1},{1,2},{2,3},{3,4},{4,5},{5,6},{6,7},{7,8},{8,9},{9,10},{10,1... | collective-permute-start | bytes 1928 | tf_op jit(solution)/shard_map/while/body/eval_jaxpr/ppermute | solution.py:15
  334.9 17.3 %collective-permute-start.1 = (bf16[160,4,128]{2,0,1:T(8,128)(2,1)S(1)}, bf16[160,4,128]{2,0,1:T(8,128)(2,1)S(1)}, u32[]{:S(2)}, u32[]{:S(2)}) collective-permute-start(bf16[160,4,128]{2,0,1:T(8,128)(2,1)S(1)} %get-tuple-element.357), channel_id=1, source_target_pairs={{0,1},{1,2},{2,3},{3,4},{4,5},{5,6},{6,7},{7,8},{8,9},{9,10},{10,1... | collective-permute-start | bytes 491528 | tf_op jit(solution)/shard_map/while/body/eval_jaxpr/ppermute | solution.py:15
  339.3 9.3 %collective-permute-start = (bf16[160,4,128]{2,0,1:T(8,128)(2,1)S(1)}, bf16[160,4,128]{2,0,1:T(8,128)(2,1)S(1)}, u32[]{:S(2)}, u32[]{:S(2)}) collective-permute-start(bf16[160,4,128]{2,0,1:T(8,128)(2,1)S(1)} %get-tuple-element.356), channel_id=1, source_target_pairs={{0,1},{1,2},{2,3},{3,4},{4,5},{5,6},{6,7},{7,8},{8,9},{9,10},{10,1... | collective-permute-start | bytes 491528 | tf_op jit(solution)/shard_map/while/body/eval_jaxpr/ppermute | solution.py:15
  355.3 8.5 %collective-permute-start.2 = (s32[160]{0:T(256)S(1)}, s32[160]{0:T(256)S(1)}, u32[]{:S(2)}, u32[]{:S(2)}) collective-permute-start(s32[160]{0:T(256)S(1)} %get-tuple-element.358), channel_id=1, source_target_pairs={{0,1},{1,2},{2,3},{3,4},{4,5},{5,6},{6,7},{7,8},{8,9},{9,10},{10,1... | collective-permute-start | bytes 1928 | tf_op jit(solution)/shard_map/while/body/eval_jaxpr/ppermute | solution.py:15
  357.5 17.3 %collective-permute-start.1 = (bf16[160,4,128]{2,0,1:T(8,128)(2,1)S(1)}, bf16[160,4,128]{2,0,1:T(8,128)(2,1)S(1)}, u32[]{:S(2)}, u32[]{:S(2)}) collective-permute-start(bf16[160,4,128]{2,0,1:T(8,128)(2,1)S(1)} %get-tuple-element.357), channel_id=1, source_target_pairs={{0,1},{1,2},{2,3},{3,4},{4,5},{5,6},{6,7},{7,8},{8,9},{9,10},{10,1... | collective-permute-start | bytes 491528 | tf_op jit(solution)/shard_map/while/body/eval_jaxpr/ppermute | solution.py:15
  361.9 9.3 %collective-permute-start = (bf16[160,4,128]{2,0,1:T(8,128)(2,1)S(1)}, bf16[160,4,128]{2,0,1:T(8,128)(2,1)S(1)}, u32[]{:S(2)}, u32[]{:S(2)}) collective-permute-start(bf16[160,4,128]{2,0,1:T(8,128)(2,1)S(1)} %get-tuple-element.356), channel_id=1, source_target_pairs={{0,1},{1,2},{2,3},{3,4},{4,5},{5,6},{6,7},{7,8},{8,9},{9,10},{10,1... | collective-permute-start | bytes 491528 | tf_op jit(solution)/shard_map/while/body/eval_jaxpr/ppermute | solution.py:15
  377.9 7.9 %collective-permute-start.2 = (s32[160]{0:T(256)S(1)}, s32[160]{0:T(256)S(1)}, u32[]{:S(2)}, u32[]{:S(2)}) collective-permute-start(s32[160]{0:T(256)S(1)} %get-tuple-element.358), channel_id=1, source_target_pairs={{0,1},{1,2},{2,3},{3,4},{4,5},{5,6},{6,7},{7,8},{8,9},{9,10},{10,1... | collective-permute-start | bytes 1928 | tf_op jit(solution)/shard_map/while/body/eval_jaxpr/ppermute | solution.py:15
  379.9 16.9 %collective-permute-start.1 = (bf16[160,4,128]{2,0,1:T(8,128)(2,1)S(1)}, bf16[160,4,128]{2,0,1:T(8,128)(2,1)S(1)}, u32[]{:S(2)}, u32[]{:S(2)}) collective-permute-start(bf16[160,4,128]{2,0,1:T(8,128)(2,1)S(1)} %get-tuple-element.357), channel_id=1, source_target_pairs={{0,1},{1,2},{2,3},{3,4},{4,5},{5,6},{6,7},{7,8},{8,9},{9,10},{10,1... | collective-permute-start | bytes 491528 | tf_op jit(solution)/shard_map/while/body/eval_jaxpr/ppermute | solution.py:15
  383.9 9.3 %collective-permute-start = (bf16[160,4,128]{2,0,1:T(8,128)(2,1)S(1)}, bf16[160,4,128]{2,0,1:T(8,128)(2,1)S(1)}, u32[]{:S(2)}, u32[]{:S(2)}) collective-permute-start(bf16[160,4,128]{2,0,1:T(8,128)(2,1)S(1)} %get-tuple-element.356), channel_id=1, source_target_pairs={{0,1},{1,2},{2,3},{3,4},{4,5},{5,6},{6,7},{7,8},{8,9},{9,10},{10,1... | collective-permute-start | bytes 491528 | tf_op jit(solution)/shard_map/while/body/eval_jaxpr/ppermute | solution.py:15
  399.9 7.9 %collective-permute-start.2 = (s32[160]{0:T(256)S(1)}, s32[160]{0:T(256)S(1)}, u32[]{:S(2)}, u32[]{:S(2)}) collective-permute-start(s32[160]{0:T(256)S(1)} %get-tuple-element.358), channel_id=1, source_target_pairs={{0,1},{1,2},{2,3},{3,4},{4,5},{5,6},{6,7},{7,8},{8,9},{9,10},{10,1... | collective-permute-start | bytes 1928 | tf_op jit(solution)/shard_map/while/body/eval_jaxpr/ppermute | solution.py:15
  401.8 16.9 %collective-permute-start.1 = (bf16[160,4,128]{2,0,1:T(8,128)(2,1)S(1)}, bf16[160,4,128]{2,0,1:T(8,128)(2,1)S(1)}, u32[]{:S(2)}, u32[]{:S(2)}) collective-permute-start(bf16[160,4,128]{2,0,1:T(8,128)(2,1)S(1)} %get-tuple-element.357), channel_id=1, source_target_pairs={{0,1},{1,2},{2,3},{3,4},{4,5},{5,6},{6,7},{7,8},{8,9},{9,10},{10,1... | collective-permute-start | bytes 491528 | tf_op jit(solution)/shard_map/while/body/eval_jaxpr/ppermute | solution.py:15
  405.9 9.3 %collective-permute-start = (bf16[160,4,128]{2,0,1:T(8,128)(2,1)S(1)}, bf16[160,4,128]{2,0,1:T(8,128)(2,1)S(1)}, u32[]{:S(2)}, u32[]{:S(2)}) collective-permute-start(bf16[160,4,128]{2,0,1:T(8,128)(2,1)S(1)} %get-tuple-element.356), channel_id=1, source_target_pairs={{0,1},{1,2},{2,3},{3,4},{4,5},{5,6},{6,7},{7,8},{8,9},{9,10},{10,1... | collective-permute-start | bytes 491528 | tf_op jit(solution)/shard_map/while/body/eval_jaxpr/ppermute | solution.py:15
  421.9 7.9 %collective-permute-start.2 = (s32[160]{0:T(256)S(1)}, s32[160]{0:T(256)S(1)}, u32[]{:S(2)}, u32[]{:S(2)}) collective-permute-start(s32[160]{0:T(256)S(1)} %get-tuple-element.358), channel_id=1, source_target_pairs={{0,1},{1,2},{2,3},{3,4},{4,5},{5,6},{6,7},{7,8},{8,9},{9,10},{10,1... | collective-permute-start | bytes 1928 | tf_op jit(solution)/shard_map/while/body/eval_jaxpr/ppermute | solution.py:15
  423.8 16.9 %collective-permute-start.1 = (bf16[160,4,128]{2,0,1:T(8,128)(2,1)S(1)}, bf16[160,4,128]{2,0,1:T(8,128)(2,1)S(1)}, u32[]{:S(2)}, u32[]{:S(2)}) collective-permute-start(bf16[160,4,128]{2,0,1:T(8,128)(2,1)S(1)} %get-tuple-element.357), channel_id=1, source_target_pairs={{0,1},{1,2},{2,3},{3,4},{4,5},{5,6},{6,7},{7,8},{8,9},{9,10},{10,1... | collective-permute-start | bytes 491528 | tf_op jit(solution)/shard_map/while/body/eval_jaxpr/ppermute | solution.py:15
  427.8 9.3 %collective-permute-start = (bf16[160,4,128]{2,0,1:T(8,128)(2,1)S(1)}, bf16[160,4,128]{2,0,1:T(8,128)(2,1)S(1)}, u32[]{:S(2)}, u32[]{:S(2)}) collective-permute-start(bf16[160,4,128]{2,0,1:T(8,128)(2,1)S(1)} %get-tuple-element.356), channel_id=1, source_target_pairs={{0,1},{1,2},{2,3},{3,4},{4,5},{5,6},{6,7},{7,8},{8,9},{9,10},{10,1... | collective-permute-start | bytes 491528 | tf_op jit(solution)/shard_map/while/body/eval_jaxpr/ppermute | solution.py:15
  443.8 9.5 %collective-permute-start.2 = (s32[160]{0:T(256)S(1)}, s32[160]{0:T(256)S(1)}, u32[]{:S(2)}, u32[]{:S(2)}) collective-permute-start(s32[160]{0:T(256)S(1)} %get-tuple-element.358), channel_id=1, source_target_pairs={{0,1},{1,2},{2,3},{3,4},{4,5},{5,6},{6,7},{7,8},{8,9},{9,10},{10,1... | collective-permute-start | bytes 1928 | tf_op jit(solution)/shard_map/while/body/eval_jaxpr/ppermute | solution.py:15
  447.0 17.8 %collective-permute-start.1 = (bf16[160,4,128]{2,0,1:T(8,128)(2,1)S(1)}, bf16[160,4,128]{2,0,1:T(8,128)(2,1)S(1)}, u32[]{:S(2)}, u32[]{:S(2)}) collective-permute-start(bf16[160,4,128]{2,0,1:T(8,128)(2,1)S(1)} %get-tuple-element.357), channel_id=1, source_target_pairs={{0,1},{1,2},{2,3},{3,4},{4,5},{5,6},{6,7},{7,8},{8,9},{9,10},{10,1... | collective-permute-start | bytes 491528 | tf_op jit(solution)/shard_map/while/body/eval_jaxpr/ppermute | solution.py:15
  451.4 9.9 %collective-permute-start = (bf16[160,4,128]{2,0,1:T(8,128)(2,1)S(1)}, bf16[160,4,128]{2,0,1:T(8,128)(2,1)S(1)}, u32[]{:S(2)}, u32[]{:S(2)}) collective-permute-start(bf16[160,4,128]{2,0,1:T(8,128)(2,1)S(1)} %get-tuple-element.356), channel_id=1, source_target_pairs={{0,1},{1,2},{2,3},{3,4},{4,5},{5,6},{6,7},{7,8},{8,9},{9,10},{10,1... | collective-permute-start | bytes 491528 | tf_op jit(solution)/shard_map/while/body/eval_jaxpr/ppermute | solution.py:15
  469.9 16.6 %collective-permute-start.1 = (bf16[160,4,128]{2,0,1:T(8,128)(2,1)S(1)}, bf16[160,4,128]{2,0,1:T(8,128)(2,1)S(1)}, u32[]{:S(2)}, u32[]{:S(2)}) collective-permute-start(bf16[160,4,128]{2,0,1:T(8,128)(2,1)S(1)} %get-tuple-element.357), channel_id=1, source_target_pairs={{0,1},{1,2},{2,3},{3,4},{4,5},{5,6},{6,7},{7,8},{8,9},{9,10},{10,1... | collective-permute-start | bytes 491528 | tf_op jit(solution)/shard_map/while/body/eval_jaxpr/ppermute | solution.py:15
  472.1 10.8 %collective-permute-start = (bf16[160,4,128]{2,0,1:T(8,128)(2,1)S(1)}, bf16[160,4,128]{2,0,1:T(8,128)(2,1)S(1)}, u32[]{:S(2)}, u32[]{:S(2)}) collective-permute-start(bf16[160,4,128]{2,0,1:T(8,128)(2,1)S(1)} %get-tuple-element.356), channel_id=1, source_target_pairs={{0,1},{1,2},{2,3},{3,4},{4,5},{5,6},{6,7},{7,8},{8,9},{9,10},{10,1... | collective-permute-start | bytes 491528 | tf_op jit(solution)/shard_map/while/body/eval_jaxpr/ppermute | solution.py:15
  489.6 7.9 %collective-permute-start.2 = (s32[160]{0:T(256)S(1)}, s32[160]{0:T(256)S(1)}, u32[]{:S(2)}, u32[]{:S(2)}) collective-permute-start(s32[160]{0:T(256)S(1)} %get-tuple-element.358), channel_id=1, source_target_pairs={{0,1},{1,2},{2,3},{3,4},{4,5},{5,6},{6,7},{7,8},{8,9},{9,10},{10,1... | collective-permute-start | bytes 1928 | tf_op jit(solution)/shard_map/while/body/eval_jaxpr/ppermute | solution.py:15
  491.5 17.5 %collective-permute-start.1 = (bf16[160,4,128]{2,0,1:T(8,128)(2,1)S(1)}, bf16[160,4,128]{2,0,1:T(8,128)(2,1)S(1)}, u32[]{:S(2)}, u32[]{:S(2)}) collective-permute-start(bf16[160,4,128]{2,0,1:T(8,128)(2,1)S(1)} %get-tuple-element.357), channel_id=1, source_target_pairs={{0,1},{1,2},{2,3},{3,4},{4,5},{5,6},{6,7},{7,8},{8,9},{9,10},{10,1... | collective-permute-start | bytes 491528 | tf_op jit(solution)/shard_map/while/body/eval_jaxpr/ppermute | solution.py:15
  494.5 11.0 %collective-permute-start = (bf16[160,4,128]{2,0,1:T(8,128)(2,1)S(1)}, bf16[160,4,128]{2,0,1:T(8,128)(2,1)S(1)}, u32[]{:S(2)}, u32[]{:S(2)}) collective-permute-start(bf16[160,4,128]{2,0,1:T(8,128)(2,1)S(1)} %get-tuple-element.356), channel_id=1, source_target_pairs={{0,1},{1,2},{2,3},{3,4},{4,5},{5,6},{6,7},{7,8},{8,9},{9,10},{10,1... | collective-permute-start | bytes 491528 | tf_op jit(solution)/shard_map/while/body/eval_jaxpr/ppermute | solution.py:15
  512.2 11.8 %collective-permute-start.2 = (s32[160]{0:T(256)S(1)}, s32[160]{0:T(256)S(1)}, u32[]{:S(2)}, u32[]{:S(2)}) collective-permute-start(s32[160]{0:T(256)S(1)} %get-tuple-element.358), channel_id=1, source_target_pairs={{0,1},{1,2},{2,3},{3,4},{4,5},{5,6},{6,7},{7,8},{8,9},{9,10},{10,1... | collective-permute-start | bytes 1928 | tf_op jit(solution)/shard_map/while/body/eval_jaxpr/ppermute | solution.py:15
  515.9 17.3 %collective-permute-start.1 = (bf16[160,4,128]{2,0,1:T(8,128)(2,1)S(1)}, bf16[160,4,128]{2,0,1:T(8,128)(2,1)S(1)}, u32[]{:S(2)}, u32[]{:S(2)}) collective-permute-start(bf16[160,4,128]{2,0,1:T(8,128)(2,1)S(1)} %get-tuple-element.357), channel_id=1, source_target_pairs={{0,1},{1,2},{2,3},{3,4},{4,5},{5,6},{6,7},{7,8},{8,9},{9,10},{10,1... | collective-permute-start | bytes 491528 | tf_op jit(solution)/shard_map/while/body/eval_jaxpr/ppermute | solution.py:15
  520.3 9.3 %collective-permute-start = (bf16[160,4,128]{2,0,1:T(8,128)(2,1)S(1)}, bf16[160,4,128]{2,0,1:T(8,128)(2,1)S(1)}, u32[]{:S(2)}, u32[]{:S(2)}) collective-permute-start(bf16[160,4,128]{2,0,1:T(8,128)(2,1)S(1)} %get-tuple-element.356), channel_id=1, source_target_pairs={{0,1},{1,2},{2,3},{3,4},{4,5},{5,6},{6,7},{7,8},{8,9},{9,10},{10,1... | collective-permute-start | bytes 491528 | tf_op jit(solution)/shard_map/while/body/eval_jaxpr/ppermute | solution.py:15
  (6 other events, 84.7 us)
Sparse Core Ops, SparseCore 0:
  87.2 71.8 reduce-scatter.1
where the time goes:
time: 548 us; the launch traced here: 546 us
  waiting for transfers between devices  182 us (33%)
  starting transfers between devices  141 us (26%)
  matrix products  101 us (18%)
  other arithmetic  52.6 us (10%)
  local copies, waits for them, and re-layouts  31.8 us (6%)
  blocking collectives  22.1 us (4%)
  between operations  13.6 us (2%)
    ppermute x48, starting transfers between devices, shifted(): return lax.ppermute(block, axis, route)  141 us
    ppermute x48, waiting for transfers between devices, shifted(): return lax.ppermute(block, axis, route)  111 us
    reduce_scatter x1, waiting for transfers between devices, local(): lax.psum_scatter(jnp.einsum('btd,dc->btc', spread, w_qkv, preferred_eleme...  70.8 us
    dot_general x17, matrix products, attend(): jnp.einsum('gjts,sgd->gjtd', expo.astype(jnp.bfloat16), value_rows, prefe...  51.1 us
    dot_general x17, matrix products, attend(): jnp.einsum('tgjd,sgd->gjts', queries, key_rows, preferred_element_type=jn...  36.8 us
    unnamed x19, local copies, waits for them, and re-layouts  25.9 us
    unnamed x1, other arithmetic  23.6 us
    all_to_all x1, blocking collectives, local(): lax.all_to_all(tokens, 'dp', split_axis=2, concat_axis=0, tiled=True)  22.1 us
  transfers between devices with their start and end apart: 49, of which 19 were waited for; matrix products, arithmetic and copies ran while one was open for 11% of the time, Pallas kernels for 0%

commit v1 on v0

--- a/solution.py
+++ b/solution.py
@@ -34,7 +34,10 @@
     tok_rows = tokens.shape[1]
     groups = QH // KVH
     score_scale = 1.0 / math.sqrt(HD)
-    spread = lax.all_to_all(tokens, "dp", split_axis=2, concat_axis=0, tiled=True)
+    spread = jnp.concatenate(
+        lax.all_to_all(jnp.stack(jnp.split(tokens, lax.axis_size("dp"), axis=2)), "dp", 0, 0),
+        axis=0,
+    )
     summed = lax.psum_scatter(
         jnp.einsum("btd,dc->btc", spread, w_qkv, preferred_element_type=jnp.float32).astype(
             jnp.bfloat16

time: 548 us -> 504 us (0.920)
  other arithmetic: 52.6 us -> 29.1 us
  local copies, waits for them, and re-layouts: 31.8 us -> 11.3 us
    unnamed x1 -> x0, other arithmetic: 23.6 us -> none
    unnamed x19 -> x14, local copies, waits for them, and re-layouts: 25.9 us -> 5.37 us
  transfers between devices with their start and end apart: 49 -> 49, of which waited for: 19 -> 19; matrix products, arithmetic and copies ran while one was open for 11% -> 12% of each run, Pallas kernels for 0% -> 0%
where the time goes in v1:
time: 504 us; the launch traced here: 502 us
  waiting for transfers between devices  182 us (36%)
  starting transfers between devices  141 us (28%)
  matrix products  101 us (20%)
  other arithmetic  29.1 us (6%)
  blocking collectives  22.1 us (4%)
  between operations  13.6 us (3%)
  local copies, waits for them, and re-layouts  11.3 us (2%)
    ppermute x48, starting transfers between devices, shifted(): return lax.ppermute(block, axis, route)  141 us
    ppermute x48, waiting for transfers between devices, shifted(): return lax.ppermute(block, axis, route)  111 us
    reduce_scatter x1, waiting for transfers between devices, local(): lax.psum_scatter(jnp.einsum('btd,dc->btc', spread, w_qkv, preferred_eleme...  70.8 us
    dot_general x17, matrix products, attend(): jnp.einsum('gjts,sgd->gjtd', expo.astype(jnp.bfloat16), value_rows, prefe...  51.1 us
    dot_general x17, matrix products, attend(): jnp.einsum('tgjd,sgd->gjts', queries, key_rows, preferred_element_type=jn...  36.8 us
    all_to_all x1, blocking collectives, local(): lax.all_to_all(jnp.stack(jnp.split(tokens, lax.axis_size('dp'), axis=2)),...  22.1 us
    reduce_sum x17, other arithmetic, attend(): new_sum = run_sum * factor + jnp.sum(expo, axis=-1)  21.1 us
    dot_general x1, matrix products, local(): jnp.einsum('btd,dc->btc', spread, w_qkv, preferred_element_type=jnp.float32)  12.9 us
  transfers between devices with their start and end apart: 49, of which 19 were waited for; matrix products, arithmetic and copies ran while one was open for 12% of the time, Pallas kernels for 0%

profile of v1, /device:TPU:72, one launch (start us, length us, event | category | flops | bytes accessed | tf_op | source)
XLA Modules:
  0.0 502.0 jit_solution(10932517947778364048)
XLA Ops:
  8.1 22.1 %all_to_all.5 = bf16[4,1,160,1024]{3,2,1,0:T(8,128)(2,1)S(1)} all-to-all(bf16[4,1,160,1024]{3,2,1,0:T(8,128)(2,1)S(1)} %pad_maximum_fusion), channel_id=1, replica_groups=mesh['dp'=4,'ctx'=64] {'dp'}, dimensions={0} | all-to-all | bytes 2621440 | tf_op jit(solution)/shard_map/all_to_all | solution.py:38
  30.2 12.9 %fusion.20 = bf16[4,160,5120]{2,1,0:T(8,128)(2,1)} fusion(bf16[1024,5120]{1,0:T(8,128)(2,1)} %param.7, bf16[4,1,160,1024]{3,2,1,0:T(8,128)(2,1)S(1)} %all_to_all.5), kind=kOutput, calls=%fused_computation.25 | convolution fusion | flops 6714163200 | bytes 18350080 | tf_op jit(solution)/shard_map/btd,dc->btc/dot_general | solution.py:42
  44.3 70.8 %reduce-scatter.2.cloned.1.call-done = bf16[1,160,5120]{2,1,0:T(8,128)(2,1)} async-done(((bf16[4,160,5120]{2,1,0:T(8,128)(2,1)}), bf16[1,160,5120]{2,1,0:T(8,128)(2,1)}) %reduce-scatter.2.cloned.1.call-update) | async-done | bytes 1638416 | tf_op jit(solution)/shard_map/reduce_scatter | solution.py:41
  130.0 362.3 %while.24 = (s32[]{:T(128)}, bf16[160,4,128]{2,0,1:T(8,128)(2,1)S(1)}, bf16[160,4,128]{2,0,1:T(8,128)(2,1)S(1)}, s32[160]{0:T(256)S(1)}, f32[4,8,160]{2,1,0:T(8,...) while((s32[]{:T(128)}, ...), condition=%wide.region_6.7_spmd.clone, body=%wide.region_3.6_spmd.clone.sunk | while | flops 429865760 | bytes 19116104 | solution.py:99
  130.2 3.4 collective-permute-start.2
  133.6 3.4 collective-permute-start.1
  137.0 3.1 collective-permute-start
  140.3 6.5 %collective-permute-done = bf16[160,4,128]{2,0,1:T(8,128)(2,1)S(1)} collective-permute-done((bf16[160,4,128]{2,0,1:T(8,128)(2,1)S(1)}, bf16[160,4,128]{2,0,1:T(8,128)(2,1)S(1)}, u32[]{:S(2)}, u32[]{:S(2)}) %collective-permute-start) | collective-permute-done | bytes 163872 | tf_op jit(solution)/shard_map/while/body/eval_jaxpr/ppermute | solution.py:15
  158.4 3.8 collective-permute-start
  162.3 5.6 %collective-permute-done = bf16[160,4,128]{2,0,1:T(8,128)(2,1)S(1)} collective-permute-done((bf16[160,4,128]{2,0,1:T(8,128)(2,1)S(1)}, bf16[160,4,128]{2,0,1:T(8,128)(2,1)S(1)}, u32[]{:S(2)}, u32[]{:S(2)}) %collective-permute-start) | collective-permute-done | bytes 163872 | tf_op jit(solution)/shard_map/while/body/eval_jaxpr/ppermute | solution.py:15
  171.5 3.1 multiply_add_fusion.5
  174.6 3.4 collective-permute-start.2
  178.0 4.4 collective-permute-start.1
  185.6 6.1 %collective-permute-done = bf16[160,4,128]{2,0,1:T(8,128)(2,1)S(1)} collective-permute-done((bf16[160,4,128]{2,0,1:T(8,128)(2,1)S(1)}, bf16[160,4,128]{2,0,1:T(8,128)(2,1)S(1)}, u32[]{:S(2)}, u32[]{:S(2)}) %collective-permute-start) | collective-permute-done | bytes 163872 | tf_op jit(solution)/shard_map/while/body/eval_jaxpr/ppermute | solution.py:15
  195.4 3.1 multiply_add_fusion.5
  200.4 4.1 collective-permute-start.1
  207.0 6.9 %collective-permute-done = bf16[160,4,128]{2,0,1:T(8,128)(2,1)S(1)} collective-permute-done((bf16[160,4,128]{2,0,1:T(8,128)(2,1)S(1)}, bf16[160,4,128]{2,0,1:T(8,128)(2,1)S(1)}, u32[]{:S(2)}, u32[]{:S(2)}) %collective-permute-start) | collective-permute-done | bytes 163872 | tf_op jit(solution)/shard_map/while/body/eval_jaxpr/ppermute | solution.py:15
  217.4 3.1 multiply_add_fusion.5
  222.4 3.4 collective-permute-start.1
  228.2 7.0 %collective-permute-done = bf16[160,4,128]{2,0,1:T(8,128)(2,1)S(1)} collective-permute-done((bf16[160,4,128]{2,0,1:T(8,128)(2,1)S(1)}, bf16[160,4,128]{2,0,1:T(8,128)(2,1)S(1)}, u32[]{:S(2)}, u32[]{:S(2)}) %collective-permute-start) | collective-permute-done | bytes 163872 | tf_op jit(solution)/shard_map/while/body/eval_jaxpr/ppermute | solution.py:15
  243.8 3.5 collective-permute-start.1
  247.3 3.5 collective-permute-start
  251.0 5.6 %collective-permute-done = bf16[160,4,128]{2,0,1:T(8,128)(2,1)S(1)} collective-permute-done((bf16[160,4,128]{2,0,1:T(8,128)(2,1)S(1)}, bf16[160,4,128]{2,0,1:T(8,128)(2,1)S(1)}, u32[]{:S(2)}, u32[]{:S(2)}) %collective-permute-start) | collective-permute-done | bytes 163872 | tf_op jit(solution)/shard_map/while/body/eval_jaxpr/ppermute | solution.py:15
  260.2 3.1 multiply_add_fusion.5
  263.3 4.4 collective-permute-start.2
  267.7 4.4 collective-permute-start.1
  274.2 7.2 %collective-permute-done = bf16[160,4,128]{2,0,1:T(8,128)(2,1)S(1)} collective-permute-done((bf16[160,4,128]{2,0,1:T(8,128)(2,1)S(1)}, bf16[160,4,128]{2,0,1:T(8,128)(2,1)S(1)}, u32[]{:S(2)}, u32[]{:S(2)}) %collective-permute-start) | collective-permute-done | bytes 163872 | tf_op jit(solution)/shard_map/while/body/eval_jaxpr/ppermute | solution.py:15
  291.0 4.4 collective-permute-start.1
  297.5 7.2 %collective-permute-done = bf16[160,4,128]{2,0,1:T(8,128)(2,1)S(1)} collective-permute-done((bf16[160,4,128]{2,0,1:T(8,128)(2,1)S(1)}, bf16[160,4,128]{2,0,1:T(8,128)(2,1)S(1)}, u32[]{:S(2)}, u32[]{:S(2)}) %collective-permute-start) | collective-permute-done | bytes 163872 | tf_op jit(solution)/shard_map/while/body/eval_jaxpr/ppermute | solution.py:15
  308.3 3.1 multiply_add_fusion.5
  313.6 4.4 collective-permute-start.1
  320.1 7.2 %collective-permute-done = bf16[160,4,128]{2,0,1:T(8,128)(2,1)S(1)} collective-permute-done((bf16[160,4,128]{2,0,1:T(8,128)(2,1)S(1)}, bf16[160,4,128]{2,0,1:T(8,128)(2,1)S(1)}, u32[]{:S(2)}, u32[]{:S(2)}) %collective-permute-start) | collective-permute-done | bytes 163872 | tf_op jit(solution)/shard_map/while/body/eval_jaxpr/ppermute | solution.py:15
  330.9 3.1 multiply_add_fusion.5
  335.9 4.0 collective-permute-start.1
  342.0 7.2 %collective-permute-done = bf16[160,4,128]{2,0,1:T(8,128)(2,1)S(1)} collective-permute-done((bf16[160,4,128]{2,0,1:T(8,128)(2,1)S(1)}, bf16[160,4,128]{2,0,1:T(8,128)(2,1)S(1)}, u32[]{:S(2)}, u32[]{:S(2)}) %collective-permute-start) | collective-permute-done | bytes 163872 | tf_op jit(solution)/shard_map/while/body/eval_jaxpr/ppermute | solution.py:15
  357.9 4.0 collective-permute-start.1
  364.0 7.2 %collective-permute-done = bf16[160,4,128]{2,0,1:T(8,128)(2,1)S(1)} collective-permute-done((bf16[160,4,128]{2,0,1:T(8,128)(2,1)S(1)}, bf16[160,4,128]{2,0,1:T(8,128)(2,1)S(1)}, u32[]{:S(2)}, u32[]{:S(2)}) %collective-permute-start) | collective-permute-done | bytes 163872 | tf_op jit(solution)/shard_map/while/body/eval_jaxpr/ppermute | solution.py:15
  379.8 4.0 collective-permute-start.1
  386.0 7.2 %collective-permute-done = bf16[160,4,128]{2,0,1:T(8,128)(2,1)S(1)} collective-permute-done((bf16[160,4,128]{2,0,1:T(8,128)(2,1)S(1)}, bf16[160,4,128]{2,0,1:T(8,128)(2,1)S(1)}, u32[]{:S(2)}, u32[]{:S(2)}) %collective-permute-start) | collective-permute-done | bytes 163872 | tf_op jit(solution)/shard_map/while/body/eval_jaxpr/ppermute | solution.py:15
  399.9 3.1 collective-permute-start.2
  403.0 4.4 collective-permute-start.1
  409.5 7.7 %collective-permute-done = bf16[160,4,128]{2,0,1:T(8,128)(2,1)S(1)} collective-permute-done((bf16[160,4,128]{2,0,1:T(8,128)(2,1)S(1)}, bf16[160,4,128]{2,0,1:T(8,128)(2,1)S(1)}, u32[]{:S(2)}, u32[]{:S(2)}) %collective-permute-start) | collective-permute-done | bytes 163872 | tf_op jit(solution)/shard_map/while/body/eval_jaxpr/ppermute | solution.py:15
  431.7 7.3 %collective-permute-done = bf16[160,4,128]{2,0,1:T(8,128)(2,1)S(1)} collective-permute-done((bf16[160,4,128]{2,0,1:T(8,128)(2,1)S(1)}, bf16[160,4,128]{2,0,1:T(8,128)(2,1)S(1)}, u32[]{:S(2)}, u32[]{:S(2)}) %collective-permute-start) | collective-permute-done | bytes 163872 | tf_op jit(solution)/shard_map/while/body/eval_jaxpr/ppermute | solution.py:15
  453.7 7.8 %collective-permute-done = bf16[160,4,128]{2,0,1:T(8,128)(2,1)S(1)} collective-permute-done((bf16[160,4,128]{2,0,1:T(8,128)(2,1)S(1)}, bf16[160,4,128]{2,0,1:T(8,128)(2,1)S(1)}, u32[]{:S(2)}, u32[]{:S(2)}) %collective-permute-start) | collective-permute-done | bytes 163872 | tf_op jit(solution)/shard_map/while/body/eval_jaxpr/ppermute | solution.py:15
  468.2 3.7 collective-permute-start.2
  471.9 4.4 collective-permute-start.1
  476.3 3.7 collective-permute-start
  480.2 5.4 %collective-permute-done = bf16[160,4,128]{2,0,1:T(8,128)(2,1)S(1)} collective-permute-done((bf16[160,4,128]{2,0,1:T(8,128)(2,1)S(1)}, bf16[160,4,128]{2,0,1:T(8,128)(2,1)S(1)}, u32[]{:S(2)}, u32[]{:S(2)}) %collective-permute-start) | collective-permute-done | bytes 163872 | tf_op jit(solution)/shard_map/while/body/eval_jaxpr/ppermute | solution.py:15
  (287 shorter events, 167.7 us)
Async XLA Ops:
  6.5 108.5 %reduce-scatter.2.cloned.1.call-start = ((), (), s32[]{:S(2)}) async-start(), calls=%async_computation.2 | async-start | bytes 8192000 | tf_op jit(solution)/shard_map/reduce_scatter | solution.py:41
  130.2 9.9 %collective-permute-start.2 = (s32[160]{0:T(256)S(1)}, s32[160]{0:T(256)S(1)}, u32[]{:S(2)}, u32[]{:S(2)}) collective-permute-start(s32[160]{0:T(256)S(1)} %get-tuple-element.352), channel_id=1, source_target_pairs={{0,1},{1,2},{2,3},{3,4},{4,5},{5,6},{6,7},{7,8},{8,9},{9,10},{10,1... | collective-permute-start | bytes 1928 | tf_op jit(solution)/shard_map/while/body/eval_jaxpr/ppermute | solution.py:15
  133.6 16.7 %collective-permute-start.1 = (bf16[160,4,128]{2,0,1:T(8,128)(2,1)S(1)}, bf16[160,4,128]{2,0,1:T(8,128)(2,1)S(1)}, u32[]{:S(2)}, u32[]{:S(2)}) collective-permute-start(bf16[160,4,128]{2,0,1:T(8,128)(2,1)S(1)} %get-tuple-element.351), channel_id=1, source_target_pairs={{0,1},{1,2},{2,3},{3,4},{4,5},{5,6},{6,7},{7,8},{8,9},{9,10},{10,1... | collective-permute-start | bytes 491528 | tf_op jit(solution)/shard_map/while/body/eval_jaxpr/ppermute | solution.py:15
  137.0 9.8 %collective-permute-start = (bf16[160,4,128]{2,0,1:T(8,128)(2,1)S(1)}, bf16[160,4,128]{2,0,1:T(8,128)(2,1)S(1)}, u32[]{:S(2)}, u32[]{:S(2)}) collective-permute-start(bf16[160,4,128]{2,0,1:T(8,128)(2,1)S(1)} %get-tuple-element.350), channel_id=1, source_target_pairs={{0,1},{1,2},{2,3},{3,4},{4,5},{5,6},{6,7},{7,8},{8,9},{9,10},{10,1... | collective-permute-start | bytes 491528 | tf_op jit(solution)/shard_map/while/body/eval_jaxpr/ppermute | solution.py:15
  153.5 8.7 %collective-permute-start.2 = (s32[160]{0:T(256)S(1)}, s32[160]{0:T(256)S(1)}, u32[]{:S(2)}, u32[]{:S(2)}) collective-permute-start(s32[160]{0:T(256)S(1)} %get-tuple-element.352), channel_id=1, source_target_pairs={{0,1},{1,2},{2,3},{3,4},{4,5},{5,6},{6,7},{7,8},{8,9},{9,10},{10,1... | collective-permute-start | bytes 1928 | tf_op jit(solution)/shard_map/while/body/eval_jaxpr/ppermute | solution.py:15
  155.4 16.1 %collective-permute-start.1 = (bf16[160,4,128]{2,0,1:T(8,128)(2,1)S(1)}, bf16[160,4,128]{2,0,1:T(8,128)(2,1)S(1)}, u32[]{:S(2)}, u32[]{:S(2)}) collective-permute-start(bf16[160,4,128]{2,0,1:T(8,128)(2,1)S(1)} %get-tuple-element.351), channel_id=1, source_target_pairs={{0,1},{1,2},{2,3},{3,4},{4,5},{5,6},{6,7},{7,8},{8,9},{9,10},{10,1... | collective-permute-start | bytes 491528 | tf_op jit(solution)/shard_map/while/body/eval_jaxpr/ppermute | solution.py:15
  158.4 9.6 %collective-permute-start = (bf16[160,4,128]{2,0,1:T(8,128)(2,1)S(1)}, bf16[160,4,128]{2,0,1:T(8,128)(2,1)S(1)}, u32[]{:S(2)}, u32[]{:S(2)}) collective-permute-start(bf16[160,4,128]{2,0,1:T(8,128)(2,1)S(1)} %get-tuple-element.350), channel_id=1, source_target_pairs={{0,1},{1,2},{2,3},{3,4},{4,5},{5,6},{6,7},{7,8},{8,9},{9,10},{10,1... | collective-permute-start | bytes 491528 | tf_op jit(solution)/shard_map/while/body/eval_jaxpr/ppermute | solution.py:15
  174.6 10.8 %collective-permute-start.2 = (s32[160]{0:T(256)S(1)}, s32[160]{0:T(256)S(1)}, u32[]{:S(2)}, u32[]{:S(2)}) collective-permute-start(s32[160]{0:T(256)S(1)} %get-tuple-element.352), channel_id=1, source_target_pairs={{0,1},{1,2},{2,3},{3,4},{4,5},{5,6},{6,7},{7,8},{8,9},{9,10},{10,1... | collective-permute-start | bytes 1928 | tf_op jit(solution)/shard_map/while/body/eval_jaxpr/ppermute | solution.py:15
  178.0 17.3 %collective-permute-start.1 = (bf16[160,4,128]{2,0,1:T(8,128)(2,1)S(1)}, bf16[160,4,128]{2,0,1:T(8,128)(2,1)S(1)}, u32[]{:S(2)}, u32[]{:S(2)}) collective-permute-start(bf16[160,4,128]{2,0,1:T(8,128)(2,1)S(1)} %get-tuple-element.351), channel_id=1, source_target_pairs={{0,1},{1,2},{2,3},{3,4},{4,5},{5,6},{6,7},{7,8},{8,9},{9,10},{10,1... | collective-permute-start | bytes 491528 | tf_op jit(solution)/shard_map/while/body/eval_jaxpr/ppermute | solution.py:15
  182.4 9.3 %collective-permute-start = (bf16[160,4,128]{2,0,1:T(8,128)(2,1)S(1)}, bf16[160,4,128]{2,0,1:T(8,128)(2,1)S(1)}, u32[]{:S(2)}, u32[]{:S(2)}) collective-permute-start(bf16[160,4,128]{2,0,1:T(8,128)(2,1)S(1)} %get-tuple-element.350), channel_id=1, source_target_pairs={{0,1},{1,2},{2,3},{3,4},{4,5},{5,6},{6,7},{7,8},{8,9},{9,10},{10,1... | collective-permute-start | bytes 491528 | tf_op jit(solution)/shard_map/while/body/eval_jaxpr/ppermute | solution.py:15
  198.4 8.4 %collective-permute-start.2 = (s32[160]{0:T(256)S(1)}, s32[160]{0:T(256)S(1)}, u32[]{:S(2)}, u32[]{:S(2)}) collective-permute-start(s32[160]{0:T(256)S(1)} %get-tuple-element.352), channel_id=1, source_target_pairs={{0,1},{1,2},{2,3},{3,4},{4,5},{5,6},{6,7},{7,8},{8,9},{9,10},{10,1... | collective-permute-start | bytes 1928 | tf_op jit(solution)/shard_map/while/body/eval_jaxpr/ppermute | solution.py:15
  200.4 17.0 %collective-permute-start.1 = (bf16[160,4,128]{2,0,1:T(8,128)(2,1)S(1)}, bf16[160,4,128]{2,0,1:T(8,128)(2,1)S(1)}, u32[]{:S(2)}, u32[]{:S(2)}) collective-permute-start(bf16[160,4,128]{2,0,1:T(8,128)(2,1)S(1)} %get-tuple-element.351), channel_id=1, source_target_pairs={{0,1},{1,2},{2,3},{3,4},{4,5},{5,6},{6,7},{7,8},{8,9},{9,10},{10,1... | collective-permute-start | bytes 491528 | tf_op jit(solution)/shard_map/while/body/eval_jaxpr/ppermute | solution.py:15
  204.5 9.3 %collective-permute-start = (bf16[160,4,128]{2,0,1:T(8,128)(2,1)S(1)}, bf16[160,4,128]{2,0,1:T(8,128)(2,1)S(1)}, u32[]{:S(2)}, u32[]{:S(2)}) collective-permute-start(bf16[160,4,128]{2,0,1:T(8,128)(2,1)S(1)} %get-tuple-element.350), channel_id=1, source_target_pairs={{0,1},{1,2},{2,3},{3,4},{4,5},{5,6},{6,7},{7,8},{8,9},{9,10},{10,1... | collective-permute-start | bytes 491528 | tf_op jit(solution)/shard_map/while/body/eval_jaxpr/ppermute | solution.py:15
  220.5 7.6 %collective-permute-start.2 = (s32[160]{0:T(256)S(1)}, s32[160]{0:T(256)S(1)}, u32[]{:S(2)}, u32[]{:S(2)}) collective-permute-start(s32[160]{0:T(256)S(1)} %get-tuple-element.352), channel_id=1, source_target_pairs={{0,1},{1,2},{2,3},{3,4},{4,5},{5,6},{6,7},{7,8},{8,9},{9,10},{10,1... | collective-permute-start | bytes 1928 | tf_op jit(solution)/shard_map/while/body/eval_jaxpr/ppermute | solution.py:15
  222.4 16.3 %collective-permute-start.1 = (bf16[160,4,128]{2,0,1:T(8,128)(2,1)S(1)}, bf16[160,4,128]{2,0,1:T(8,128)(2,1)S(1)}, u32[]{:S(2)}, u32[]{:S(2)}) collective-permute-start(bf16[160,4,128]{2,0,1:T(8,128)(2,1)S(1)} %get-tuple-element.351), channel_id=1, source_target_pairs={{0,1},{1,2},{2,3},{3,4},{4,5},{5,6},{6,7},{7,8},{8,9},{9,10},{10,1... | collective-permute-start | bytes 491528 | tf_op jit(solution)/shard_map/while/body/eval_jaxpr/ppermute | solution.py:15
  225.9 9.3 %collective-permute-start = (bf16[160,4,128]{2,0,1:T(8,128)(2,1)S(1)}, bf16[160,4,128]{2,0,1:T(8,128)(2,1)S(1)}, u32[]{:S(2)}, u32[]{:S(2)}) collective-permute-start(bf16[160,4,128]{2,0,1:T(8,128)(2,1)S(1)} %get-tuple-element.350), channel_id=1, source_target_pairs={{0,1},{1,2},{2,3},{3,4},{4,5},{5,6},{6,7},{7,8},{8,9},{9,10},{10,1... | collective-permute-start | bytes 491528 | tf_op jit(solution)/shard_map/while/body/eval_jaxpr/ppermute | solution.py:15
  241.9 8.9 %collective-permute-start.2 = (s32[160]{0:T(256)S(1)}, s32[160]{0:T(256)S(1)}, u32[]{:S(2)}, u32[]{:S(2)}) collective-permute-start(s32[160]{0:T(256)S(1)} %get-tuple-element.352), channel_id=1, source_target_pairs={{0,1},{1,2},{2,3},{3,4},{4,5},{5,6},{6,7},{7,8},{8,9},{9,10},{10,1... | collective-permute-start | bytes 1928 | tf_op jit(solution)/shard_map/while/body/eval_jaxpr/ppermute | solution.py:15
  243.8 16.4 %collective-permute-start.1 = (bf16[160,4,128]{2,0,1:T(8,128)(2,1)S(1)}, bf16[160,4,128]{2,0,1:T(8,128)(2,1)S(1)}, u32[]{:S(2)}, u32[]{:S(2)}) collective-permute-start(bf16[160,4,128]{2,0,1:T(8,128)(2,1)S(1)} %get-tuple-element.351), channel_id=1, source_target_pairs={{0,1},{1,2},{2,3},{3,4},{4,5},{5,6},{6,7},{7,8},{8,9},{9,10},{10,1... | collective-permute-start | bytes 491528 | tf_op jit(solution)/shard_map/while/body/eval_jaxpr/ppermute | solution.py:15
  247.3 9.3 %collective-permute-start = (bf16[160,4,128]{2,0,1:T(8,128)(2,1)S(1)}, bf16[160,4,128]{2,0,1:T(8,128)(2,1)S(1)}, u32[]{:S(2)}, u32[]{:S(2)}) collective-permute-start(bf16[160,4,128]{2,0,1:T(8,128)(2,1)S(1)} %get-tuple-element.350), channel_id=1, source_target_pairs={{0,1},{1,2},{2,3},{3,4},{4,5},{5,6},{6,7},{7,8},{8,9},{9,10},{10,1... | collective-permute-start | bytes 491528 | tf_op jit(solution)/shard_map/while/body/eval_jaxpr/ppermute | solution.py:15
  263.3 10.8 %collective-permute-start.2 = (s32[160]{0:T(256)S(1)}, s32[160]{0:T(256)S(1)}, u32[]{:S(2)}, u32[]{:S(2)}) collective-permute-start(s32[160]{0:T(256)S(1)} %get-tuple-element.352), channel_id=1, source_target_pairs={{0,1},{1,2},{2,3},{3,4},{4,5},{5,6},{6,7},{7,8},{8,9},{9,10},{10,1... | collective-permute-start | bytes 1928 | tf_op jit(solution)/shard_map/while/body/eval_jaxpr/ppermute | solution.py:15
  267.7 17.3 %collective-permute-start.1 = (bf16[160,4,128]{2,0,1:T(8,128)(2,1)S(1)}, bf16[160,4,128]{2,0,1:T(8,128)(2,1)S(1)}, u32[]{:S(2)}, u32[]{:S(2)}) collective-permute-start(bf16[160,4,128]{2,0,1:T(8,128)(2,1)S(1)} %get-tuple-element.351), channel_id=1, source_target_pairs={{0,1},{1,2},{2,3},{3,4},{4,5},{5,6},{6,7},{7,8},{8,9},{9,10},{10,1... | collective-permute-start | bytes 491528 | tf_op jit(solution)/shard_map/while/body/eval_jaxpr/ppermute | solution.py:15
  272.1 9.3 %collective-permute-start = (bf16[160,4,128]{2,0,1:T(8,128)(2,1)S(1)}, bf16[160,4,128]{2,0,1:T(8,128)(2,1)S(1)}, u32[]{:S(2)}, u32[]{:S(2)}) collective-permute-start(bf16[160,4,128]{2,0,1:T(8,128)(2,1)S(1)} %get-tuple-element.350), channel_id=1, source_target_pairs={{0,1},{1,2},{2,3},{3,4},{4,5},{5,6},{6,7},{7,8},{8,9},{9,10},{10,1... | collective-permute-start | bytes 491528 | tf_op jit(solution)/shard_map/while/body/eval_jaxpr/ppermute | solution.py:15
  288.1 9.2 %collective-permute-start.2 = (s32[160]{0:T(256)S(1)}, s32[160]{0:T(256)S(1)}, u32[]{:S(2)}, u32[]{:S(2)}) collective-permute-start(s32[160]{0:T(256)S(1)} %get-tuple-element.352), channel_id=1, source_target_pairs={{0,1},{1,2},{2,3},{3,4},{4,5},{5,6},{6,7},{7,8},{8,9},{9,10},{10,1... | collective-permute-start | bytes 1928 | tf_op jit(solution)/shard_map/while/body/eval_jaxpr/ppermute | solution.py:15
  291.0 17.3 %collective-permute-start.1 = (bf16[160,4,128]{2,0,1:T(8,128)(2,1)S(1)}, bf16[160,4,128]{2,0,1:T(8,128)(2,1)S(1)}, u32[]{:S(2)}, u32[]{:S(2)}) collective-permute-start(bf16[160,4,128]{2,0,1:T(8,128)(2,1)S(1)} %get-tuple-element.351), channel_id=1, source_target_pairs={{0,1},{1,2},{2,3},{3,4},{4,5},{5,6},{6,7},{7,8},{8,9},{9,10},{10,1... | collective-permute-start | bytes 491528 | tf_op jit(solution)/shard_map/while/body/eval_jaxpr/ppermute | solution.py:15
  295.4 9.3 %collective-permute-start = (bf16[160,4,128]{2,0,1:T(8,128)(2,1)S(1)}, bf16[160,4,128]{2,0,1:T(8,128)(2,1)S(1)}, u32[]{:S(2)}, u32[]{:S(2)}) collective-permute-start(bf16[160,4,128]{2,0,1:T(8,128)(2,1)S(1)} %get-tuple-element.350), channel_id=1, source_target_pairs={{0,1},{1,2},{2,3},{3,4},{4,5},{5,6},{6,7},{7,8},{8,9},{9,10},{10,1... | collective-permute-start | bytes 491528 | tf_op jit(solution)/shard_map/while/body/eval_jaxpr/ppermute | solution.py:15
  311.4 8.6 %collective-permute-start.2 = (s32[160]{0:T(256)S(1)}, s32[160]{0:T(256)S(1)}, u32[]{:S(2)}, u32[]{:S(2)}) collective-permute-start(s32[160]{0:T(256)S(1)} %get-tuple-element.352), channel_id=1, source_target_pairs={{0,1},{1,2},{2,3},{3,4},{4,5},{5,6},{6,7},{7,8},{8,9},{9,10},{10,1... | collective-permute-start | bytes 1928 | tf_op jit(solution)/shard_map/while/body/eval_jaxpr/ppermute | solution.py:15
  313.6 17.3 %collective-permute-start.1 = (bf16[160,4,128]{2,0,1:T(8,128)(2,1)S(1)}, bf16[160,4,128]{2,0,1:T(8,128)(2,1)S(1)}, u32[]{:S(2)}, u32[]{:S(2)}) collective-permute-start(bf16[160,4,128]{2,0,1:T(8,128)(2,1)S(1)} %get-tuple-element.351), channel_id=1, source_target_pairs={{0,1},{1,2},{2,3},{3,4},{4,5},{5,6},{6,7},{7,8},{8,9},{9,10},{10,1... | collective-permute-start | bytes 491528 | tf_op jit(solution)/shard_map/while/body/eval_jaxpr/ppermute | solution.py:15
  317.9 9.3 %collective-permute-start = (bf16[160,4,128]{2,0,1:T(8,128)(2,1)S(1)}, bf16[160,4,128]{2,0,1:T(8,128)(2,1)S(1)}, u32[]{:S(2)}, u32[]{:S(2)}) collective-permute-start(bf16[160,4,128]{2,0,1:T(8,128)(2,1)S(1)} %get-tuple-element.350), channel_id=1, source_target_pairs={{0,1},{1,2},{2,3},{3,4},{4,5},{5,6},{6,7},{7,8},{8,9},{9,10},{10,1... | collective-permute-start | bytes 491528 | tf_op jit(solution)/shard_map/while/body/eval_jaxpr/ppermute | solution.py:15
  333.9 7.9 %collective-permute-start.2 = (s32[160]{0:T(256)S(1)}, s32[160]{0:T(256)S(1)}, u32[]{:S(2)}, u32[]{:S(2)}) collective-permute-start(s32[160]{0:T(256)S(1)} %get-tuple-element.352), channel_id=1, source_target_pairs={{0,1},{1,2},{2,3},{3,4},{4,5},{5,6},{6,7},{7,8},{8,9},{9,10},{10,1... | collective-permute-start | bytes 1928 | tf_op jit(solution)/shard_map/while/body/eval_jaxpr/ppermute | solution.py:15
  335.9 16.9 %collective-permute-start.1 = (bf16[160,4,128]{2,0,1:T(8,128)(2,1)S(1)}, bf16[160,4,128]{2,0,1:T(8,128)(2,1)S(1)}, u32[]{:S(2)}, u32[]{:S(2)}) collective-permute-start(bf16[160,4,128]{2,0,1:T(8,128)(2,1)S(1)} %get-tuple-element.351), channel_id=1, source_target_pairs={{0,1},{1,2},{2,3},{3,4},{4,5},{5,6},{6,7},{7,8},{8,9},{9,10},{10,1... | collective-permute-start | bytes 491528 | tf_op jit(solution)/shard_map/while/body/eval_jaxpr/ppermute | solution.py:15
  339.9 9.3 %collective-permute-start = (bf16[160,4,128]{2,0,1:T(8,128)(2,1)S(1)}, bf16[160,4,128]{2,0,1:T(8,128)(2,1)S(1)}, u32[]{:S(2)}, u32[]{:S(2)}) collective-permute-start(bf16[160,4,128]{2,0,1:T(8,128)(2,1)S(1)} %get-tuple-element.350), channel_id=1, source_target_pairs={{0,1},{1,2},{2,3},{3,4},{4,5},{5,6},{6,7},{7,8},{8,9},{9,10},{10,1... | collective-permute-start | bytes 491528 | tf_op jit(solution)/shard_map/while/body/eval_jaxpr/ppermute | solution.py:15
  355.9 7.9 %collective-permute-start.2 = (s32[160]{0:T(256)S(1)}, s32[160]{0:T(256)S(1)}, u32[]{:S(2)}, u32[]{:S(2)}) collective-permute-start(s32[160]{0:T(256)S(1)} %get-tuple-element.352), channel_id=1, source_target_pairs={{0,1},{1,2},{2,3},{3,4},{4,5},{5,6},{6,7},{7,8},{8,9},{9,10},{10,1... | collective-permute-start | bytes 1928 | tf_op jit(solution)/shard_map/while/body/eval_jaxpr/ppermute | solution.py:15
  357.9 16.9 %collective-permute-start.1 = (bf16[160,4,128]{2,0,1:T(8,128)(2,1)S(1)}, bf16[160,4,128]{2,0,1:T(8,128)(2,1)S(1)}, u32[]{:S(2)}, u32[]{:S(2)}) collective-permute-start(bf16[160,4,128]{2,0,1:T(8,128)(2,1)S(1)} %get-tuple-element.351), channel_id=1, source_target_pairs={{0,1},{1,2},{2,3},{3,4},{4,5},{5,6},{6,7},{7,8},{8,9},{9,10},{10,1... | collective-permute-start | bytes 491528 | tf_op jit(solution)/shard_map/while/body/eval_jaxpr/ppermute | solution.py:15
  361.9 9.3 %collective-permute-start = (bf16[160,4,128]{2,0,1:T(8,128)(2,1)S(1)}, bf16[160,4,128]{2,0,1:T(8,128)(2,1)S(1)}, u32[]{:S(2)}, u32[]{:S(2)}) collective-permute-start(bf16[160,4,128]{2,0,1:T(8,128)(2,1)S(1)} %get-tuple-element.350), channel_id=1, source_target_pairs={{0,1},{1,2},{2,3},{3,4},{4,5},{5,6},{6,7},{7,8},{8,9},{9,10},{10,1... | collective-permute-start | bytes 491528 | tf_op jit(solution)/shard_map/while/body/eval_jaxpr/ppermute | solution.py:15
  377.9 7.9 %collective-permute-start.2 = (s32[160]{0:T(256)S(1)}, s32[160]{0:T(256)S(1)}, u32[]{:S(2)}, u32[]{:S(2)}) collective-permute-start(s32[160]{0:T(256)S(1)} %get-tuple-element.352), channel_id=1, source_target_pairs={{0,1},{1,2},{2,3},{3,4},{4,5},{5,6},{6,7},{7,8},{8,9},{9,10},{10,1... | collective-permute-start | bytes 1928 | tf_op jit(solution)/shard_map/while/body/eval_jaxpr/ppermute | solution.py:15
  379.8 16.9 %collective-permute-start.1 = (bf16[160,4,128]{2,0,1:T(8,128)(2,1)S(1)}, bf16[160,4,128]{2,0,1:T(8,128)(2,1)S(1)}, u32[]{:S(2)}, u32[]{:S(2)}) collective-permute-start(bf16[160,4,128]{2,0,1:T(8,128)(2,1)S(1)} %get-tuple-element.351), channel_id=1, source_target_pairs={{0,1},{1,2},{2,3},{3,4},{4,5},{5,6},{6,7},{7,8},{8,9},{9,10},{10,1... | collective-permute-start | bytes 491528 | tf_op jit(solution)/shard_map/while/body/eval_jaxpr/ppermute | solution.py:15
  383.9 9.3 %collective-permute-start = (bf16[160,4,128]{2,0,1:T(8,128)(2,1)S(1)}, bf16[160,4,128]{2,0,1:T(8,128)(2,1)S(1)}, u32[]{:S(2)}, u32[]{:S(2)}) collective-permute-start(bf16[160,4,128]{2,0,1:T(8,128)(2,1)S(1)} %get-tuple-element.350), channel_id=1, source_target_pairs={{0,1},{1,2},{2,3},{3,4},{4,5},{5,6},{6,7},{7,8},{8,9},{9,10},{10,1... | collective-permute-start | bytes 491528 | tf_op jit(solution)/shard_map/while/body/eval_jaxpr/ppermute | solution.py:15
  399.9 9.5 %collective-permute-start.2 = (s32[160]{0:T(256)S(1)}, s32[160]{0:T(256)S(1)}, u32[]{:S(2)}, u32[]{:S(2)}) collective-permute-start(s32[160]{0:T(256)S(1)} %get-tuple-element.352), channel_id=1, source_target_pairs={{0,1},{1,2},{2,3},{3,4},{4,5},{5,6},{6,7},{7,8},{8,9},{9,10},{10,1... | collective-permute-start | bytes 1928 | tf_op jit(solution)/shard_map/while/body/eval_jaxpr/ppermute | solution.py:15
  403.0 17.8 %collective-permute-start.1 = (bf16[160,4,128]{2,0,1:T(8,128)(2,1)S(1)}, bf16[160,4,128]{2,0,1:T(8,128)(2,1)S(1)}, u32[]{:S(2)}, u32[]{:S(2)}) collective-permute-start(bf16[160,4,128]{2,0,1:T(8,128)(2,1)S(1)} %get-tuple-element.351), channel_id=1, source_target_pairs={{0,1},{1,2},{2,3},{3,4},{4,5},{5,6},{6,7},{7,8},{8,9},{9,10},{10,1... | collective-permute-start | bytes 491528 | tf_op jit(solution)/shard_map/while/body/eval_jaxpr/ppermute | solution.py:15
  407.4 9.9 %collective-permute-start = (bf16[160,4,128]{2,0,1:T(8,128)(2,1)S(1)}, bf16[160,4,128]{2,0,1:T(8,128)(2,1)S(1)}, u32[]{:S(2)}, u32[]{:S(2)}) collective-permute-start(bf16[160,4,128]{2,0,1:T(8,128)(2,1)S(1)} %get-tuple-element.350), channel_id=1, source_target_pairs={{0,1},{1,2},{2,3},{3,4},{4,5},{5,6},{6,7},{7,8},{8,9},{9,10},{10,1... | collective-permute-start | bytes 491528 | tf_op jit(solution)/shard_map/while/body/eval_jaxpr/ppermute | solution.py:15
  425.9 16.6 %collective-permute-start.1 = (bf16[160,4,128]{2,0,1:T(8,128)(2,1)S(1)}, bf16[160,4,128]{2,0,1:T(8,128)(2,1)S(1)}, u32[]{:S(2)}, u32[]{:S(2)}) collective-permute-start(bf16[160,4,128]{2,0,1:T(8,128)(2,1)S(1)} %get-tuple-element.351), channel_id=1, source_target_pairs={{0,1},{1,2},{2,3},{3,4},{4,5},{5,6},{6,7},{7,8},{8,9},{9,10},{10,1... | collective-permute-start | bytes 491528 | tf_op jit(solution)/shard_map/while/body/eval_jaxpr/ppermute | solution.py:15
  428.2 10.8 %collective-permute-start = (bf16[160,4,128]{2,0,1:T(8,128)(2,1)S(1)}, bf16[160,4,128]{2,0,1:T(8,128)(2,1)S(1)}, u32[]{:S(2)}, u32[]{:S(2)}) collective-permute-start(bf16[160,4,128]{2,0,1:T(8,128)(2,1)S(1)} %get-tuple-element.350), channel_id=1, source_target_pairs={{0,1},{1,2},{2,3},{3,4},{4,5},{5,6},{6,7},{7,8},{8,9},{9,10},{10,1... | collective-permute-start | bytes 491528 | tf_op jit(solution)/shard_map/while/body/eval_jaxpr/ppermute | solution.py:15
  445.6 7.9 %collective-permute-start.2 = (s32[160]{0:T(256)S(1)}, s32[160]{0:T(256)S(1)}, u32[]{:S(2)}, u32[]{:S(2)}) collective-permute-start(s32[160]{0:T(256)S(1)} %get-tuple-element.352), channel_id=1, source_target_pairs={{0,1},{1,2},{2,3},{3,4},{4,5},{5,6},{6,7},{7,8},{8,9},{9,10},{10,1... | collective-permute-start | bytes 1928 | tf_op jit(solution)/shard_map/while/body/eval_jaxpr/ppermute | solution.py:15
  447.6 17.5 %collective-permute-start.1 = (bf16[160,4,128]{2,0,1:T(8,128)(2,1)S(1)}, bf16[160,4,128]{2,0,1:T(8,128)(2,1)S(1)}, u32[]{:S(2)}, u32[]{:S(2)}) collective-permute-start(bf16[160,4,128]{2,0,1:T(8,128)(2,1)S(1)} %get-tuple-element.351), channel_id=1, source_target_pairs={{0,1},{1,2},{2,3},{3,4},{4,5},{5,6},{6,7},{7,8},{8,9},{9,10},{10,1... | collective-permute-start | bytes 491528 | tf_op jit(solution)/shard_map/while/body/eval_jaxpr/ppermute | solution.py:15
  450.6 11.0 %collective-permute-start = (bf16[160,4,128]{2,0,1:T(8,128)(2,1)S(1)}, bf16[160,4,128]{2,0,1:T(8,128)(2,1)S(1)}, u32[]{:S(2)}, u32[]{:S(2)}) collective-permute-start(bf16[160,4,128]{2,0,1:T(8,128)(2,1)S(1)} %get-tuple-element.350), channel_id=1, source_target_pairs={{0,1},{1,2},{2,3},{3,4},{4,5},{5,6},{6,7},{7,8},{8,9},{9,10},{10,1... | collective-permute-start | bytes 491528 | tf_op jit(solution)/shard_map/while/body/eval_jaxpr/ppermute | solution.py:15
  468.2 11.8 %collective-permute-start.2 = (s32[160]{0:T(256)S(1)}, s32[160]{0:T(256)S(1)}, u32[]{:S(2)}, u32[]{:S(2)}) collective-permute-start(s32[160]{0:T(256)S(1)} %get-tuple-element.352), channel_id=1, source_target_pairs={{0,1},{1,2},{2,3},{3,4},{4,5},{5,6},{6,7},{7,8},{8,9},{9,10},{10,1... | collective-permute-start | bytes 1928 | tf_op jit(solution)/shard_map/while/body/eval_jaxpr/ppermute | solution.py:15
  471.9 17.3 %collective-permute-start.1 = (bf16[160,4,128]{2,0,1:T(8,128)(2,1)S(1)}, bf16[160,4,128]{2,0,1:T(8,128)(2,1)S(1)}, u32[]{:S(2)}, u32[]{:S(2)}) collective-permute-start(bf16[160,4,128]{2,0,1:T(8,128)(2,1)S(1)} %get-tuple-element.351), channel_id=1, source_target_pairs={{0,1},{1,2},{2,3},{3,4},{4,5},{5,6},{6,7},{7,8},{8,9},{9,10},{10,1... | collective-permute-start | bytes 491528 | tf_op jit(solution)/shard_map/while/body/eval_jaxpr/ppermute | solution.py:15
  476.3 9.3 %collective-permute-start = (bf16[160,4,128]{2,0,1:T(8,128)(2,1)S(1)}, bf16[160,4,128]{2,0,1:T(8,128)(2,1)S(1)}, u32[]{:S(2)}, u32[]{:S(2)}) collective-permute-start(bf16[160,4,128]{2,0,1:T(8,128)(2,1)S(1)} %get-tuple-element.350), channel_id=1, source_target_pairs={{0,1},{1,2},{2,3},{3,4},{4,5},{5,6},{6,7},{7,8},{8,9},{9,10},{10,1... | collective-permute-start | bytes 491528 | tf_op jit(solution)/shard_map/while/body/eval_jaxpr/ppermute | solution.py:15
  (6 other events, 84.7 us)
Sparse Core Ops, SparseCore 0:
  43.2 71.7 reduce-scatter.1
